TPU v7x, 256 devices: a whole 4x4x8 slice. The times are simulated.
256 devices in a mesh: ex: 16 (over z_hi, y, core), feat: 16 (over x, z_lo).
Axes of the slice: x: 4, y: 4, z: 8 (z_hi: 2, z_lo: 4; z = z_hi * 4 + z_lo), core: 2. Of those that a mesh axis runs over, the one named last changes fastest.
Arguments:
- activations: bfloat16 [6144, 28672], P('ex', 'feat'), may hold values from -13 to 13
- out_grads: bfloat16 [6144, 8192], P('ex', 'feat'), may hold values from -13 to 13
- lengths: int32 [16], P('ex'), may hold values from 96 to 384, as said below
Outputs:
- kernel: float32 [16, 16], P('ex')
Inputs may be any that keep to these rules, and one draw needn't show every extreme that they name: `lengths`: each sequence has at least 96 valid tokens, and some sequence is full.
All inputs are finite; a program needn't handle non-finite values.
Results may differ from a plain program's by a relative error of at most 0.0003.
Values may be sent and summed in bfloat16 or wider, within the bound.
A program may use at most 64 MiB of HBM per device.

v0:
```python
import jax
import jax.numpy as jnp
from jax import lax
from jax.sharding import PartitionSpec as P

FF = 28672
D = 8192
LEN = 384


def passed_along(value, axis, steps):
    count = lax.axis_size(axis)
    pairs = [(source, (source + steps) % count) for source in range(count)]
    return lax.ppermute(value, axis, pairs)


def per_device(activations, out_grads, lengths):
    seq_count = lengths.shape[0]
    tok_count = activations.shape[0]
    seq_len = tok_count // seq_count
    feat_count = lax.axis_size("feat")
    ex_count = lax.axis_size("ex")
    half_count = ex_count // 2
    row_count = tok_count // feat_count
    grads_split = out_grads.reshape(seq_count, seq_len, out_grads.shape[1])
    valid = jnp.arange(seq_len, dtype=jnp.int32)[None, :] < lengths[:, None]
    masked = jnp.where(valid[:, :, None], grads_split, jnp.zeros_like(grads_split)).reshape(
        out_grads.shape
    )
    begin_own = lax.axis_index("feat") * row_count
    row_seq = (begin_own + jnp.arange(row_count, dtype=jnp.int32)) // seq_len
    onehot = (row_seq[:, None] == jnp.arange(seq_count, dtype=jnp.int32)[None, :]).astype(
        jnp.float32
    )
    contract = (((1,), (1,)), ((), ()))
    partials = []
    partner = (activations, masked)
    for step in range(half_count + 1):
        if step > 0:
            partner = passed_along((partner[0], partner[1]), "ex", 1)
        partner_acts, partner_grads = partner
        act_gram = lax.dot_general(
            activations, partner_acts, contract, preferred_element_type=jnp.float32
        )
        grad_gram = lax.dot_general(
            masked, partner_grads, contract, preferred_element_type=jnp.float32
        )
        shares = lax.psum_scatter(
            jnp.concatenate([act_gram, grad_gram], axis=1), "feat", scatter_dimension=0, tiled=True
        )
        product = shares[:, :tok_count] * shares[:, tok_count:]
        colsum = product.reshape(row_count, seq_count, seq_len).sum(axis=2)
        partials.append(jnp.dot(onehot.T, colsum, precision=lax.Precision.HIGHEST))
    pair_values = jnp.stack([lax.psum(piece, "feat") for piece in partials])
    pair_values = pair_values / float(LEN * FF * D)
    tables_all = lax.all_gather(pair_values[None], "ex", axis=0, tiled=True)
    my_index = lax.axis_index("ex")
    others = jnp.arange(ex_count, dtype=jnp.int32)
    distance = jnp.mod(my_index - others, ex_count)
    back_dist = jnp.mod(others - my_index, ex_count)
    own_tiles = tables_all[my_index]
    forward = own_tiles[jnp.clip(distance, 0, half_count)]
    mirrored = tables_all[others, jnp.clip(back_dist, 0, half_count)]
    mirrored = jnp.swapaxes(mirrored, 1, 2)
    chosen = jnp.where((distance <= half_count)[:, None, None], forward, mirrored)
    return jnp.transpose(chosen, (1, 0, 2)).reshape(seq_count, ex_count * seq_count)


def solution(mesh):
    placed = (P("ex", "feat"), P("ex", "feat"), P("ex"))
    return jax.shard_map(
        per_device, mesh=mesh, in_specs=placed, out_specs=P("ex", None), check_vma=False
    )
```

profile of v0, /device:TPU:1, one launch (start us, length us, event | category | flops | bytes accessed | tf_op | source)
XLA Modules:
  0.0 1000.2 jit_solution(16837338516794123431)
XLA Ops:
  7.3 1.1 broadcast_select_fusion
  8.8 0.9 fusion.20
  9.8 1.4 copy.22
  11.3 2.8 collective-permute-start
  14.2 19.4 %collective-permute-done.1 = bf16[384,512]{1,0:T(8,128)(2,1)S(1)} collective-permute-done((bf16[384,512]{1,0:T(8,128)(2,1)S(1)}, bf16[384,512]{1,0:T(8,128)(2,1)S(1)}, u32[]{:S(2)}, u32[]{:S(2)}) %collective-permute-start.1) | collective-permute-done | bytes 393248 | tf_op jit(solution)/shard_map/ppermute | solution.py:14
  34.0 1.1 copy-done.11
  35.0 0.9 fusion.22
  36.0 1.4 copy.24
  37.5 2.6 collective-permute-start.2
  40.1 19.7 %collective-permute-done.3 = bf16[384,512]{1,0:T(8,128)(2,1)S(1)} collective-permute-done((bf16[384,512]{1,0:T(8,128)(2,1)S(1)}, bf16[384,512]{1,0:T(8,128)(2,1)S(1)}, u32[]{:S(2)}, u32[]{:S(2)}) %collective-permute-start.3) | collective-permute-done | bytes 393248 | tf_op jit(solution)/shard_map/ppermute | solution.py:14
  60.5 1.1 copy-done.6
  61.6 0.9 fusion.24
  62.6 1.4 copy.26
  64.0 2.2 collective-permute-start.4
  66.3 47.9 %collective-permute-done.5 = bf16[384,512]{1,0:T(8,128)(2,1)S(1)} collective-permute-done((bf16[384,512]{1,0:T(8,128)(2,1)S(1)}, bf16[384,512]{1,0:T(8,128)(2,1)S(1)}, u32[]{:S(2)}, u32[]{:S(2)}) %collective-permute-start.5) | collective-permute-done | bytes 393248 | tf_op jit(solution)/shard_map/ppermute | solution.py:14
  114.9 1.1 copy-done.7
  116.0 0.9 fusion.26
  117.0 1.4 copy.28
  118.6 36.8 %collective-permute-done.7 = bf16[384,512]{1,0:T(8,128)(2,1)S(1)} collective-permute-done((bf16[384,512]{1,0:T(8,128)(2,1)S(1)}, bf16[384,512]{1,0:T(8,128)(2,1)S(1)}, u32[]{:S(2)}, u32[]{:S(2)}) %collective-permute-start.7) | collective-permute-done | bytes 393248 | tf_op jit(solution)/shard_map/ppermute | solution.py:14
  156.1 1.1 copy-done.8
  157.2 0.9 fusion.28
  158.2 1.4 copy.30
  160.0 53.6 %collective-permute-done.9 = bf16[384,512]{1,0:T(8,128)(2,1)S(1)} collective-permute-done((bf16[384,512]{1,0:T(8,128)(2,1)S(1)}, bf16[384,512]{1,0:T(8,128)(2,1)S(1)}, u32[]{:S(2)}, u32[]{:S(2)}) %collective-permute-start.9) | collective-permute-done | bytes 393248 | tf_op jit(solution)/shard_map/ppermute | solution.py:14
  214.4 1.1 copy-done.9
  215.4 0.9 fusion.30
  216.4 1.5 copy.32
  218.1 39.5 %collective-permute-done.11 = bf16[384,512]{1,0:T(8,128)(2,1)S(1)} collective-permute-done((bf16[384,512]{1,0:T(8,128)(2,1)S(1)}, bf16[384,512]{1,0:T(8,128)(2,1)S(1)}, u32[]{:S(2)}, u32[]{:S(2)}) %collective-permute-start.11) | collective-permute-done | bytes 393248 | tf_op jit(solution)/shard_map/ppermute | solution.py:14
  258.4 1.1 copy-done.10
  259.5 0.9 fusion.32
  260.5 1.4 copy.34
  262.1 46.4 %collective-permute-done.13 = bf16[384,512]{1,0:T(8,128)(2,1)S(1)} collective-permute-done((bf16[384,512]{1,0:T(8,128)(2,1)S(1)}, bf16[384,512]{1,0:T(8,128)(2,1)S(1)}, u32[]{:S(2)}, u32[]{:S(2)}) %collective-permute-start.13) | collective-permute-done | bytes 393248 | tf_op jit(solution)/shard_map/ppermute | solution.py:14
  309.3 1.1 copy-done.5
  310.4 0.9 fusion.34
  311.3 1.4 copy.36
  313.1 0.8 fusion.19
  314.8 47.3 %collective-permute-done.15 = bf16[384,512]{1,0:T(8,128)(2,1)S(1)} collective-permute-done((bf16[384,512]{1,0:T(8,128)(2,1)S(1)}, bf16[384,512]{1,0:T(8,128)(2,1)S(1)}, u32[]{:S(2)}, u32[]{:S(2)}) %collective-permute-start.15) | collective-permute-done | bytes 393248 | tf_op jit(solution)/shard_map/ppermute | solution.py:14
  362.5 0.8 fusion.18
  363.6 2.2 fusion.36
  365.9 1.4 copy.38
  369.2 95.8 %reduce-scatter.34.cloned.1.call-done = f32[24,768]{1,0:T(8,128)} async-done(((f32[384,768]{1,0:T(8,128)}), f32[24,768]{1,0:T(8,128)}) %reduce-scatter.34.cloned.1.call-update) | async-done | bytes 73744
  466.1 92.2 %reduce-scatter.36.cloned.1.call-done = f32[24,768]{1,0:T(8,128)} async-done(((f32[384,768]{1,0:T(8,128)}), f32[24,768]{1,0:T(8,128)}) %reduce-scatter.36.cloned.1.call-update) | async-done | bytes 73744
  560.2 83.8 %reduce-scatter.38.cloned.1.call-done = f32[24,768]{1,0:T(8,128)} async-done(((f32[384,768]{1,0:T(8,128)}), f32[24,768]{1,0:T(8,128)}) %reduce-scatter.38.cloned.1.call-update) | async-done | bytes 73744
  645.1 83.7 %reduce-scatter.40.cloned.1.call-done = f32[24,768]{1,0:T(8,128)} async-done(((f32[384,768]{1,0:T(8,128)}), f32[24,768]{1,0:T(8,128)}) %reduce-scatter.40.cloned.1.call-update) | async-done | bytes 73744
  730.7 84.3 %reduce-scatter.42.cloned.1.call-done = f32[24,768]{1,0:T(8,128)} async-done(((f32[384,768]{1,0:T(8,128)}), f32[24,768]{1,0:T(8,128)}) %reduce-scatter.42.cloned.1.call-update) | async-done | bytes 73744
  816.0 85.7 %reduce-scatter.44.cloned.1.call-done = f32[24,768]{1,0:T(8,128)} async-done(((f32[384,768]{1,0:T(8,128)}), f32[24,768]{1,0:T(8,128)}) %reduce-scatter.44.cloned.1.call-update) | async-done | bytes 73744
  903.6 33.5 %all-reduce = (f32[1,1,1,1]{1,3,2,0:T(1,128)}, f32[1,1,1,1]{1,3,2,0:T(1,128)}, f32[1,1,1,1]{1,3,2,0:T(1,128)}, f32[1,1,1,1]{1,3,2,0:T(1,128)}, f32[1,1,1,1]{1,3,...) all-reduce(f32[1,1,1,1]{1,3,2,0:T(1,128)} %bitcast.1, ...), channel_id=1, replica_groups=mesh['ex'=16,'feat'=16] {'feat'}, use_global_device_ids=true, to_apply=%region_2.3 | all-reduce | flops 9 | bytes 72 | tf_op jit(solution)/shard_map/psum | solution.py:54
  937.1 5.7 stack.39
  942.8 49.0 %all_gather.3 = f32[16,9,1,1]{1,3,2,0:T(1,128)S(1)} all-gather(f32[1,9,1,1]{1,3,2,0:T(1,128)S(1)} %broadcast_multiply_fusion), channel_id=1, replica_groups=mesh['ex'=16,'feat'=16] {'ex'}, dimensions={0}, use_global_device_ids=true | all-gather | bytes 612 | tf_op jit(solution)/shard_map/all_gather | solution.py:56
  (124 shorter events, 21.5 us)
Async XLA Ops:
  6.5 2.3 copy-start
  6.5 306.5 %reduce-scatter.28.cloned.1.call-start = ((), (), s32[]{:S(2)}) async-start(), calls=%async_computation.9 | async-start | bytes 1253376
  11.3 351.2 %reduce-scatter.30.cloned.1.call-start = ((), (), s32[]{:S(2)}) async-start(), calls=%async_computation.10 | async-start | bytes 1253376
  11.3 22.6 %collective-permute-start = (bf16[384,1792]{1,0:T(8,128)(2,1)S(1)}, bf16[384,1792]{1,0:T(8,128)(2,1)S(1)}, u32[]{:S(2)}, u32[]{:S(2)}) collective-permute-start(bf16[384,1792]{1,0:T(8,128)(2,1)S(1)} %copy-done), channel_id=1, source_target_pairs={{0,16},{16,32},{32,48},{48,64},{64,80},{80,96},{96,112},{112,128},... | collective-permute-start | bytes 4128776 | tf_op jit(solution)/shard_map/ppermute | solution.py:14
  14.1 19.5 %collective-permute-start.1 = (bf16[384,512]{1,0:T(8,128)(2,1)S(1)}, bf16[384,512]{1,0:T(8,128)(2,1)S(1)}, u32[]{:S(2)}, u32[]{:S(2)}) collective-permute-start(bf16[384,512]{1,0:T(8,128)(2,1)S(1)} %broadcast_select_fusion), channel_id=1, source_target_pairs={{0,16},{16,32},{32,48},{48,64},{64,80},{80,96},{96,112},{112,128},... | collective-permute-start | bytes 1179656 | tf_op jit(solution)/shard_map/ppermute | solution.py:14
  33.9 1.1 copy-start.11
  37.4 24.2 %copy-start.1 = (bf16[384,1792]{1,0:T(8,128)(2,1)S(1)}, bf16[384,1792]{1,0:T(8,128)(2,1)}, u32[]{:S(2)}) copy-start(bf16[384,1792]{1,0:T(8,128)(2,1)} %param.3) | copy-start | bytes 4128772
  37.4 330.0 %reduce-scatter.32.cloned.1.call-start = ((), (), s32[]{:S(2)}) async-start(), calls=%async_computation.11 | async-start | bytes 1253376
  37.5 23.0 %collective-permute-start.2 = (bf16[384,1792]{1,0:T(8,128)(2,1)}, bf16[384,1792]{1,0:T(8,128)(2,1)S(1)}, u32[]{:S(2)}, u32[]{:S(2)}) collective-permute-start(bf16[384,1792]{1,0:T(8,128)(2,1)} %copy-done.11), channel_id=1, source_target_pairs={{0,16},{16,32},{32,48},{48,64},{64,80},{80,96},{96,112},{112,128},... | collective-permute-start | bytes 4128776 | tf_op jit(solution)/shard_map/ppermute | solution.py:14
  40.0 19.7 %collective-permute-start.3 = (bf16[384,512]{1,0:T(8,128)(2,1)S(1)}, bf16[384,512]{1,0:T(8,128)(2,1)S(1)}, u32[]{:S(2)}, u32[]{:S(2)}) collective-permute-start(bf16[384,512]{1,0:T(8,128)(2,1)S(1)} %collective-permute-done.1), channel_id=1, source_target_pairs={{0,16},{16,32},{32,48},{48,64},{64,80},{80,96},{96,112},{112,128},... | collective-permute-start | bytes 1179656 | tf_op jit(solution)/shard_map/ppermute | solution.py:14
  60.5 1.1 copy-start.6
  64.0 401.0 %reduce-scatter.34.cloned.1.call-start = ((), (), s32[]{:S(2)}) async-start(), calls=%async_computation.12 | async-start | bytes 1253376
  64.0 50.9 %collective-permute-start.4 = (bf16[384,1792]{1,0:T(8,128)(2,1)}, bf16[384,1792]{1,0:T(8,128)(2,1)S(1)}, u32[]{:S(2)}, u32[]{:S(2)}) collective-permute-start(bf16[384,1792]{1,0:T(8,128)(2,1)} %copy-done.6), channel_id=1, source_target_pairs={{0,16},{16,32},{32,48},{48,64},{64,80},{80,96},{96,112},{112,128},... | collective-permute-start | bytes 4128776 | tf_op jit(solution)/shard_map/ppermute | solution.py:14
  66.2 48.0 %collective-permute-start.5 = (bf16[384,512]{1,0:T(8,128)(2,1)S(1)}, bf16[384,512]{1,0:T(8,128)(2,1)S(1)}, u32[]{:S(2)}, u32[]{:S(2)}) collective-permute-start(bf16[384,512]{1,0:T(8,128)(2,1)S(1)} %collective-permute-done.3), channel_id=1, source_target_pairs={{0,16},{16,32},{32,48},{48,64},{64,80},{80,96},{96,112},{112,128},... | collective-permute-start | bytes 1179656 | tf_op jit(solution)/shard_map/ppermute | solution.py:14
  114.9 1.1 copy-start.7
  118.4 38.8 %copy-start.2 = (bf16[384,1792]{1,0:T(8,128)(2,1)S(1)}, bf16[384,1792]{1,0:T(8,128)(2,1)}, u32[]{:S(2)}) copy-start(bf16[384,1792]{1,0:T(8,128)(2,1)} %param.3) | copy-start | bytes 4128772
  118.4 439.9 %reduce-scatter.36.cloned.1.call-start = ((), (), s32[]{:S(2)}) async-start(), calls=%async_computation.13 | async-start | bytes 1253376
  118.4 37.7 %collective-permute-start.6 = (bf16[384,1792]{1,0:T(8,128)(2,1)}, bf16[384,1792]{1,0:T(8,128)(2,1)S(1)}, u32[]{:S(2)}, u32[]{:S(2)}) collective-permute-start(bf16[384,1792]{1,0:T(8,128)(2,1)} %copy-done.7), channel_id=1, source_target_pairs={{0,16},{16,32},{32,48},{48,64},{64,80},{80,96},{96,112},{112,128},... | collective-permute-start | bytes 4128776 | tf_op jit(solution)/shard_map/ppermute | solution.py:14
  118.5 36.9 %collective-permute-start.7 = (bf16[384,512]{1,0:T(8,128)(2,1)S(1)}, bf16[384,512]{1,0:T(8,128)(2,1)S(1)}, u32[]{:S(2)}, u32[]{:S(2)}) collective-permute-start(bf16[384,512]{1,0:T(8,128)(2,1)S(1)} %collective-permute-done.5), channel_id=1, source_target_pairs={{0,16},{16,32},{32,48},{48,64},{64,80},{80,96},{96,112},{112,128},... | collective-permute-start | bytes 1179656 | tf_op jit(solution)/shard_map/ppermute | solution.py:14
  156.1 1.1 copy-start.8
  159.6 484.3 %reduce-scatter.38.cloned.1.call-start = ((), (), s32[]{:S(2)}) async-start(), calls=%async_computation.14 | async-start | bytes 1253376
  159.7 54.7 %collective-permute-start.8 = (bf16[384,1792]{1,0:T(8,128)(2,1)}, bf16[384,1792]{1,0:T(8,128)(2,1)S(1)}, u32[]{:S(2)}, u32[]{:S(2)}) collective-permute-start(bf16[384,1792]{1,0:T(8,128)(2,1)} %copy-done.8), channel_id=1, source_target_pairs={{0,16},{16,32},{32,48},{48,64},{64,80},{80,96},{96,112},{112,128},... | collective-permute-start | bytes 4128776 | tf_op jit(solution)/shard_map/ppermute | solution.py:14
  160.0 53.7 %collective-permute-start.9 = (bf16[384,512]{1,0:T(8,128)(2,1)S(1)}, bf16[384,512]{1,0:T(8,128)(2,1)S(1)}, u32[]{:S(2)}, u32[]{:S(2)}) collective-permute-start(bf16[384,512]{1,0:T(8,128)(2,1)S(1)} %collective-permute-done.7), channel_id=1, source_target_pairs={{0,16},{16,32},{32,48},{48,64},{64,80},{80,96},{96,112},{112,128},... | collective-permute-start | bytes 1179656 | tf_op jit(solution)/shard_map/ppermute | solution.py:14
  214.4 1.1 copy-start.9
  217.9 41.6 %copy-start.3 = (bf16[384,1792]{1,0:T(8,128)(2,1)S(1)}, bf16[384,1792]{1,0:T(8,128)(2,1)}, u32[]{:S(2)}) copy-start(bf16[384,1792]{1,0:T(8,128)(2,1)} %param.3) | copy-start | bytes 4128772
  217.9 510.9 %reduce-scatter.40.cloned.1.call-start = ((), (), s32[]{:S(2)}) async-start(), calls=%async_computation.15 | async-start | bytes 1253376
  218.0 40.4 %collective-permute-start.10 = (bf16[384,1792]{1,0:T(8,128)(2,1)}, bf16[384,1792]{1,0:T(8,128)(2,1)S(1)}, u32[]{:S(2)}, u32[]{:S(2)}) collective-permute-start(bf16[384,1792]{1,0:T(8,128)(2,1)} %copy-done.9), channel_id=1, source_target_pairs={{0,16},{16,32},{32,48},{48,64},{64,80},{80,96},{96,112},{112,128},... | collective-permute-start | bytes 4128776 | tf_op jit(solution)/shard_map/ppermute | solution.py:14
  218.1 39.6 %collective-permute-start.11 = (bf16[384,512]{1,0:T(8,128)(2,1)S(1)}, bf16[384,512]{1,0:T(8,128)(2,1)S(1)}, u32[]{:S(2)}, u32[]{:S(2)}) collective-permute-start(bf16[384,512]{1,0:T(8,128)(2,1)S(1)} %collective-permute-done.9), channel_id=1, source_target_pairs={{0,16},{16,32},{32,48},{48,64},{64,80},{80,96},{96,112},{112,128},... | collective-permute-start | bytes 1179656 | tf_op jit(solution)/shard_map/ppermute | solution.py:14
  258.4 1.1 copy-start.10
  261.9 48.5 %copy-start.4 = (bf16[384,1792]{1,0:T(8,128)(2,1)S(1)}, bf16[384,1792]{1,0:T(8,128)(2,1)}, u32[]{:S(2)}) copy-start(bf16[384,1792]{1,0:T(8,128)(2,1)} %param.3) | copy-start | bytes 4128772
  261.9 553.0 %reduce-scatter.42.cloned.1.call-start = ((), (), s32[]{:S(2)}) async-start(), calls=%async_computation.16 | async-start | bytes 1253376
  262.0 47.3 %collective-permute-start.12 = (bf16[384,1792]{1,0:T(8,128)(2,1)}, bf16[384,1792]{1,0:T(8,128)(2,1)S(1)}, u32[]{:S(2)}, u32[]{:S(2)}) collective-permute-start(bf16[384,1792]{1,0:T(8,128)(2,1)} %copy-done.10), channel_id=1, source_target_pairs={{0,16},{16,32},{32,48},{48,64},{64,80},{80,96},{96,112},{112,128},... | collective-permute-start | bytes 4128776 | tf_op jit(solution)/shard_map/ppermute | solution.py:14
  262.0 46.5 %collective-permute-start.13 = (bf16[384,512]{1,0:T(8,128)(2,1)S(1)}, bf16[384,512]{1,0:T(8,128)(2,1)S(1)}, u32[]{:S(2)}, u32[]{:S(2)}) collective-permute-start(bf16[384,512]{1,0:T(8,128)(2,1)S(1)} %collective-permute-done.11), channel_id=1, source_target_pairs={{0,16},{16,32},{32,48},{48,64},{64,80},{80,96},{96,112},{112,128},... | collective-permute-start | bytes 1179656 | tf_op jit(solution)/shard_map/ppermute | solution.py:14
  309.3 1.1 copy-start.5
  312.7 589.0 %reduce-scatter.44.cloned.1.call-start = ((), (), s32[]{:S(2)}) async-start(), calls=%async_computation.17 | async-start | bytes 1253376
  312.8 50.8 %collective-permute-start.14 = (bf16[384,1792]{1,0:T(8,128)(2,1)}, bf16[384,1792]{1,0:T(8,128)(2,1)}, u32[]{:S(2)}, u32[]{:S(2)}) collective-permute-start(bf16[384,1792]{1,0:T(8,128)(2,1)} %copy-done.5), channel_id=1, source_target_pairs={{0,16},{16,32},{32,48},{48,64},{64,80},{80,96},{96,112},{112,128},... | collective-permute-start | bytes 4128776 | tf_op jit(solution)/shard_map/ppermute | solution.py:14
  312.9 49.1 %collective-permute-start.15 = (bf16[384,512]{1,0:T(8,128)(2,1)S(1)}, bf16[384,512]{1,0:T(8,128)(2,1)S(1)}, u32[]{:S(2)}, u32[]{:S(2)}) collective-permute-start(bf16[384,512]{1,0:T(8,128)(2,1)S(1)} %collective-permute-done.13), channel_id=1, source_target_pairs={{0,16},{16,32},{32,48},{48,64},{64,80},{80,96},{96,112},{112,128},... | collective-permute-start | bytes 1179656 | tf_op jit(solution)/shard_map/ppermute | solution.py:14
Sparse Core Ops, SparseCore 0:
  11.4 81.3 reduce-scatter.27
  95.3 107.1 reduce-scatter.29
  205.0 124.1 reduce-scatter.31
  331.5 133.3 reduce-scatter.33
  467.4 90.9 reduce-scatter.35
  560.7 83.2 reduce-scatter.37
  646.5 82.2 reduce-scatter.39
  731.4 83.5 reduce-scatter.41
  817.5 84.2 reduce-scatter.43
where the time goes:
time: 1000 us
  waiting for transfers between devices  838 us (84%)
  blocking collectives  82.5 us (8%)
  local copies, waits for them, and re-layouts  36.8 us (4%)
  between operations  14.5 us (1%)
  matrix products  12.8 us (1%)
    unnamed x18, waiting for transfers between devices  526 us
    ppermute x16, waiting for transfers between devices, passed_along(): return lax.ppermute(value, axis, pairs)  312 us
    all_gather x1, blocking collectives, per_device(): tables_all = lax.all_gather(pair_values[None], 'ex', axis=0, tiled=True)  49 us
    psum x1, blocking collectives, per_device(): pair_values = jnp.stack([lax.psum(piece, 'feat') for piece in partials])  33.5 us
    unnamed x51, local copies, waits for them, and re-layouts  22.6 us
  transfers between devices with their start and end apart: 25, of which 20 were waited for; matrix products, arithmetic and copies ran while one was open for 3% of the time, Pallas kernels for 0%

commit v1 on v0

v1 whole, which is shorter than its diff:
```python
import jax
import jax.numpy as jnp
from jax import lax
from jax.experimental import pallas as pl
from jax.experimental.pallas import tpu as pltpu
from jax.sharding import PartitionSpec as P

FF = 28672
D = 8192
LEN = 384
SEQS = 16

MESH = pl.DeviceIdType.MESH
AH = FF // 32
GH = D // 32
WH = AH + GH
CH = 128
QR = CH // 4
UNITS = 37
SAMES = 13
LAG = 4
NT = (((1,), (1,)), ((), ()))


def device(h, y, c, x, l):
    return {"ex": (h * 4 + y) * 2 + c, "feat": x * 4 + l}


def bytes_wait(ref, sem):
    pltpu.make_async_copy(ref, ref, sem).wait()


def pick(index, values):
    out = values[-1]
    for i in range(len(values) - 2, -1, -1):
        out = jnp.where(index == i, values[i], out)
    return out


def body(act_ref, grad_ref, len_ref, out_ref, w, graw, xp, xq, rp, rq, sp2, sq2, rp2, rq2,
         zs, zr, zc, tb, in_sem, sib_s, sib_r, far_s, far_r, y_s, y_r, fw_s, fw_r, rf_s, rf_r,
         x1_s, x1_r, x2_s, x2_r, z_s, z_r, c_r, t_s, t_r):
    e = lax.axis_index("ex")
    f = lax.axis_index("feat")
    h, y, c = e // 8, (e // 2) % 4, e % 2
    x, l = f // 4, f % 4
    zz = h * 4 + l
    own = 4 + 2 * c
    up, down = (y + 1) % 4, (y + 3) % 4
    sgn = 1 - 2 * c
    qa, qb = ((x + 1) // 2) % 2, x // 2
    xa, xb = x + 1 - 2 * (x % 2), 3 - x
    c2 = jnp.where(y < 2, c, 1 - c)

    loads = []
    for half in range(2):
        loads.append(pltpu.make_async_copy(
            act_ref.at[:, pl.ds(half * AH, AH)], w.at[own + half, :, pl.ds(0, AH)],
            in_sem.at[half]))
    loads.append(pltpu.make_async_copy(grad_ref, graw, in_sem.at[2]))
    for ld in loads:
        ld.start()

    def other_side(t, k):
        o_shift = jnp.where(t == 0, 0, jnp.where(t == 1, 1, jnp.where(t == 2, 3, 4 - sgn)))
        y2 = jnp.where(t == 3, y + o_shift + 4 - (1 - 2 * k), y + o_shift) % 4
        t2 = jnp.where(t == 1, 2, jnp.where(t == 2, 1, t))
        return y2, t2

    kept = (c + h) % 2

    bar = pltpu.get_barrier_semaphore()

    def greet(dev):
        pl.semaphore_signal(bar, inc=1, device_id=dev, device_id_type=MESH)

    def plane(i):
        return device(h, i % 4, c, i // 4, l)

    def column(i):
        return device(i // 8, y, i % 2, x, (i // 2) % 4)

    in_plane, in_column = x * 4 + y, zz * 2 + c
    for d in range(1, 16):
        greet(plane((in_plane + d) % 16))
        greet(column((in_column + d) % 16))
    ysrc, _ = other_side(l, kept)
    for l2 in range(4):
        greet(device(1 - h, ysrc, kept, x, l2))

    for ld in loads:
        ld.wait()
    rows = lax.broadcasted_iota(jnp.int32, (LEN, GH), 0)
    valid = rows < len_ref[0]
    for half in range(2):
        g = graw[:, half * GH:(half + 1) * GH].astype(jnp.float32)
        w[own + half, :, AH:WH] = jnp.where(valid, g, 0.0).astype(jnp.bfloat16)
    pl.semaphore_wait(bar, 34)

    def start(src, dst, send, recv, dev):
        pltpu.make_async_remote_copy(src_ref=src, dst_ref=dst, send_sem=send, recv_sem=recv,
                                     device_id=dev, device_id_type=MESH).start()

    def chunk(j):
        return pl.ds(pl.multiple_of(j * CH, CH), CH)

    sibling = device(h, y, 1 - c, x, l)

    def send_far(j):
        start(w.at[own + 1 - h, chunk(j)], w.at[12, chunk(j)], far_s.at[j], far_r.at[j],
              device(1 - h, y, c, x, l))

    def send_near(j):
        start(w.at[pl.ds(own, 2), chunk(j)], w.at[pl.ds(8 + 2 * c, 2), chunk(j)],
              y_s.at[j, 0], y_r.at[j, 0], device(h, down, c, x, l))
        start(w.at[pl.ds(own, 2), chunk(j)], w.at[pl.ds(2 * c, 2), chunk(j)],
              y_s.at[j, 1], y_r.at[j, 1], device(h, up, c, x, l))

    for j in range(2):
        send_far(j)
        send_near(j)
    start(w.at[pl.ds(own, 2)], w.at[pl.ds(own, 2)], sib_s, sib_r, sibling)

    def arrive(j):
        for s in range(2):
            bytes_wait(w.at[pl.ds((8 if s == 0 else 0) + 2 * c, 2), chunk(j)], y_r.at[j, s])

        @pl.when(j < 1)
        def _():
            send_near(j + 2)

        for s in range(2):
            slot = pl.ds((8 if s == 0 else 0) + 2 * c, 2)
            start(w.at[slot, chunk(j)], w.at[slot, chunk(j)], fw_s.at[j, s], fw_r.at[j, s], sibling)
        bytes_wait(w.at[12, chunk(j)], far_r.at[j])

        @pl.when(j < 1)
        def _():
            send_far(j + 2)

        start(w.at[12, chunk(j)], w.at[13, chunk(j)], rf_s.at[j], rf_r.at[j],
              device(h, jnp.where(c == 0, down, up), c, x, l))
        for s in range(2):
            slot = pl.ds((8 if s == 0 else 0) + 2 * (1 - c), 2)
            bytes_wait(w.at[slot, chunk(j)], fw_r.at[j, s])

    def stage_of(p):
        j = jnp.where(p < 8, 0, jnp.where(p < 17, 1, 2))
        return j, jnp.where(p > 32, p - 33, p - pick(j, (4, 8, 15)))

    def corner(p):
        late = p > 34
        return (jnp.where(p < 17, p - 12, jnp.where(late, 0, (p - 17) // 2)),
                jnp.where(p < 17, 0, jnp.where(late, p - 34, 1 + (p - 19) % 2)))

    def in_stage(p):
        return ((p >= 4) & (p < 12)) | (p == 17) | (p == 18) | (p == 33) | (p == 34)

    def in_corner(p):
        return ((p >= 12) & (p < 17)) | ((p >= 19) & (p < 27)) | (p > 34)

    def cross_of(p):
        j, q = stage_of(p)
        v, u = corner(p)
        m = p - 27
        st, co = in_stage(p), in_corner(p)
        t = jnp.where(st, 0, jnp.where(co, (v + 1) // 2, 3))
        k = jnp.where(st, q - 2, jnp.where(co, (v + 1) % 2, m // 3))
        return t, k, jnp.where(st, j, jnp.where(co, u, m % 3))

    def is_cross(p):
        return (in_stage(p) & (stage_of(p)[1] >= 2)) | (in_corner(p) & (corner(p)[0] > 0)) | (
            (p > 26) & (p < 33))

    def same_of(p):
        j, q = stage_of(p)
        return jnp.where(p < 4, p, jnp.where(in_stage(p), 4 + 2 * j + q, 10 + corner(p)[1]))

    def unit_of_same(s):
        j, q = (s - 4) // 2, (s - 4) % 2
        return jnp.where(s < 4, s, jnp.where(s < 10, pick(j, (4, 8, 33)) + q,
                                             pick(s - 10, (12, 35, 36))))

    def multiply(p):
        cross = is_cross(p)
        j, q = stage_of(p)
        v, u = corner(p)
        t, k, part = cross_of(p)
        st, co = in_stage(p), in_corner(p)
        left = jnp.where(p < 2, own, jnp.where(p < 4, 4, jnp.where(st, own, 2 * c)))
        right = jnp.where(p < 2, own, jnp.where(p < 4, 6, jnp.where(st, 8 + 2 * q, 8 + 2 * c2)))
        o = 2 * (pick(t, (2, 4, 0, 4 * c)) + k) + h
        r = jnp.where(t == 3, 13, 12)
        left = jnp.where(cross, jnp.where(h == 0, o, r), left)
        right = jnp.where(cross, jnp.where(h == 0, r, o), right)
        row_wise = cross & (t == 0) & (h == 1)
        col = jnp.where(p == 2, c, jnp.where(p == 3, 2, jnp.where(st, j, p - 27) % 3))
        us = pick(u, (0, 1, 2))
        for b in range(3):
            ib = jnp.where(row_wise, j, b)
            jb = jnp.where(row_wise, b, col)
            ib = jnp.where(co, pick(us, ((0, 1, 1)[b], (0, 0, 1)[b], 2)), ib)
            jb = jnp.where(co, pick(us, ((1, 0, 1)[b], (0, 2, 2)[b], b)), jb)
            ib = jnp.where(p == 0, b, jnp.where(p == 1, (1, 2, 2)[b], ib))
            jb = jnp.where(p == 0, b, jnp.where(p == 1, (0, 0, 1)[b], jb))

            def gram(half, c0, c1):
                return lax.dot_general(w[left + half, chunk(ib), c0:c1], w[right + half, chunk(jb), c0:c1],
                                       NT, preferred_element_type=jnp.float32)

            def store(pa, qg):
                pa, qg = pa.astype(jnp.bfloat16), qg.astype(jnp.bfloat16)
                for a in range(2):
                    for bb in range(2):
                        sl = slice((2 * a + bb) * QR, (2 * a + bb + 1) * QR)
                        xp[p, a, bb, b] = pa[sl]
                        xq[p, bb, a, b] = qg[sl]

            @pl.when(cross)
            def _():
                store(gram(0, 0, AH), gram(0, AH, WH))

            @pl.when(jnp.logical_not(cross))
            def _():
                store(gram(0, 0, AH) + gram(1, 0, AH), gram(0, AH, WH) + gram(1, AH, WH))

        start(xp.at[p, 1 - qa], rp.at[p], x1_s.at[0], x1_r.at[p, 0], device(h, y, c, xa, l))
        start(xq.at[p, 1 - qb], rq.at[p], x1_s.at[1], x1_r.at[p, 1], device(h, y, c, xb, l))

    def f32(v):
        return v.astype(jnp.float32)

    def exchange(p):
        bytes_wait(rp.at[p], x1_r.at[p, 0])
        sp2[p] = (f32(xp[p, qa, 1 - qb]) + f32(rp[p, 1 - qb])).astype(jnp.bfloat16)
        start(sp2.at[p], rp2.at[p], x2_s.at[0], x2_r.at[p, 0], device(h, y, c, xb, l))
        bytes_wait(rq.at[p], x1_r.at[p, 1])
        sq2[p] = (f32(xq[p, qb, 1 - qa]) + f32(rq[p, 1 - qa])).astype(jnp.bfloat16)
        start(sq2.at[p], rq2.at[p], x2_s.at[1], x2_r.at[p, 1], device(h, y, c, xa, l))

    def finish(p):
        bytes_wait(rp2.at[p], x2_r.at[p, 0])
        zs[p, :, :, 0:CH] = (f32(xp[p, qa, qb]) + f32(rp[p, qb]) + f32(rp2[p])).astype(jnp.bfloat16)
        bytes_wait(rq2.at[p], x2_r.at[p, 1])
        zs[p, :, :, CH:2 * CH] = (f32(xq[p, qb, qa]) + f32(rq[p, qa]) + f32(rq2[p])).astype(jnp.bfloat16)
        cross = is_cross(p)
        s = same_of(p)
        t, k, part = cross_of(p)
        mine = k == kept

        @pl.when(jnp.logical_not(cross) & (s % 4 != l))
        def _():
            o = s % 4
            start(zs.at[p], zr.at[s, (l - o + 3) % 4], z_s.at[p], z_r.at[s],
                  device(h, y, c, x, o))

        @pl.when(cross & mine & (t == l))
        def _():
            zc[zz, part] = zs[p]

        @pl.when(cross & jnp.logical_not(mine & (t == l)))
        def _():
            y2, t2 = other_side(t, k)
            dev = device(jnp.where(mine, h, 1 - h), jnp.where(mine, y, y2),
                         jnp.where(mine, c, k), x, jnp.where(mine, t, t2))
            start(zs.at[p], zc.at[zz, part], z_s.at[p], c_r, dev)

    row_id = lax.broadcasted_iota(jnp.int32, (SEQS, 128), 0)
    col_id = lax.broadcasted_iota(jnp.int32, (SEQS, 128), 1)

    def put(value, b, s):
        hit = ((row_id == b) & (col_id == s)) | ((row_id == s) & (col_id == b))
        return jnp.where(hit, value, 0.0)

    def seq(hh, yy, cc):
        return (hh * 4 + yy) * 2 + cc

    def keep_same(s):
        p = unit_of_same(s)

        @pl.when(s % 4 == l)
        def _():
            bytes_wait(zr.at[s], z_r.at[s])
            total = f32(zs[p])
            for d in range(3):
                total = total + f32(zr[s, d])
            value = jnp.sum(total[:, :, 0:CH] * total[:, :, CH:2 * CH])
            value = value * jnp.where(s == 1, 2.0, jnp.where(s == 3, 0.5, 1.0))
            b = jnp.where(s < 2, e, jnp.where(s < 4, seq(h, y, 0), jnp.where(
                s < 10, e, seq(h, down, c))))
            b2 = jnp.where(s < 2, e, jnp.where(s < 4, seq(h, y, 1), jnp.where(
                s < 10, seq(h, up, s % 2), seq(h, up, c2))))
            tb[0, in_plane] = tb[0, in_plane] + put(value, b, b2)

    tb[0, in_plane] = jnp.zeros((SEQS, 128), jnp.float32)

    @pl.loop(0, UNITS)
    def _(p):
        @pl.when(p == 2)
        def _():
            bytes_wait(w.at[pl.ds(own, 2)], sib_r)

        @pl.when(p == 4)
        def _():
            @pl.loop(0, 4)
            def _(i):
                exchange(p - 4 + i)

            @pl.loop(0, 4)
            def _(i):
                finish(p - 4 + i)

        @pl.when((p == 4) | (p == 8) | (p == 17))
        def _():
            arrive(stage_of(p)[0])

        @pl.when(p == 27)
        def _():
            for j in range(3):
                bytes_wait(w.at[13, chunk(j)], rf_r.at[j])

        multiply(p)

        @pl.when(p >= 4 + LAG)
        def _():
            exchange(p - LAG)

        @pl.when(p >= 4 + 2 * LAG)
        def _():
            finish(p - 2 * LAG)

        @pl.when(p == UNITS - 3)
        def _():
            @pl.loop(0, 8)
            def _(s):
                keep_same(s)

    @pl.loop(UNITS, UNITS + 2 * LAG)
    def _(p):
        @pl.when(p < UNITS + LAG)
        def _():
            exchange(p - LAG)

        finish(p - 2 * LAG)

    bytes_wait(zc.at[pl.ds(0, 7)], c_r)
    o_y = jnp.where(l == 0, y, jnp.where(l == 1, up, jnp.where(l == 2, down, (y + 4 - sgn) % 4)))
    r_y = jnp.where(l == 3, (y + 4 + sgn) % 4, y)

    def cross_block(i, acc):
        a, b = i // 3, i % 3
        a2, b2 = jnp.where(l == 0, b, a), jnp.where(l == 0, a, b)
        total = jnp.zeros((QR, 2 * CH), jnp.float32)
        for src in range(4):
            total = total + f32(zc[src, a2, b2])
        for src in range(4, 8):
            total = total + f32(zc[src, a, b])
        return acc + total[:, 0:CH] * total[:, CH:2 * CH]

    acc = lax.fori_loop(0, 9, cross_block, jnp.zeros((QR, CH), jnp.float32))
    tb[0, in_plane] = tb[0, in_plane] + put(
        jnp.sum(acc), seq(h, o_y, kept), seq(1 - h, r_y, c))

    @pl.loop(8, SAMES)
    def _(s):
        keep_same(s)

    def add_up(s, me, dev_of):
        for d in range(1, 16):
            start(tb.at[s, me], tb.at[s, me], t_s.at[s], t_r.at[s], dev_of((me + d) % 16))
        bytes_wait(tb.at[s, pl.ds(0, 15)], t_r.at[s])
        total = tb[s, 0]
        for d in range(1, 16):
            total = total + tb[s, d]
        return total

    tb[1, in_column] = add_up(0, in_plane, plane)
    total = add_up(1, in_column, column)
    line = jnp.sum(jnp.where(row_id == e, total, 0.0), axis=0, keepdims=True)
    out_ref[...] = line[:, 0:SEQS] / float(LEN * FF * D)

    bytes_wait(w.at[pl.ds(0, 2)], sib_s)
    for j in range(3):
        bytes_wait(w.at[0, chunk(j)], far_s.at[j])
        bytes_wait(w.at[0, chunk(j)], rf_s.at[j])
        for s in range(2):
            bytes_wait(w.at[pl.ds(0, 2), chunk(j)], y_s.at[j, s])
            bytes_wait(w.at[pl.ds(0, 2), chunk(j)], fw_s.at[j, s])
    for s in range(2):
        bytes_wait(tb.at[s, pl.ds(0, 15)], t_s.at[s])
    bytes_wait(rp, x1_s.at[0])
    bytes_wait(rq, x1_s.at[1])
    bytes_wait(rp2, x2_s.at[0])
    bytes_wait(rq2, x2_s.at[1])

    @pl.loop(0, UNITS)
    def _(p):
        t, k, _ = cross_of(p)
        here = jnp.where(is_cross(p), (k == kept) & (t == l), same_of(p) % 4 == l)

        @pl.when(jnp.logical_not(here))
        def _():
            bytes_wait(zs.at[p], z_s.at[p])


def per_device(activations, out_grads, lengths):
    bf, dma = jnp.bfloat16, pltpu.SemaphoreType.DMA
    return pl.pallas_call(
        body,
        out_shape=jax.ShapeDtypeStruct((1, SEQS), jnp.float32),
        in_specs=[pl.BlockSpec(memory_space=pl.ANY), pl.BlockSpec(memory_space=pl.ANY),
                  pl.BlockSpec(memory_space=pltpu.SMEM)],
        out_specs=pl.BlockSpec(memory_space=pltpu.VMEM),
        scratch_shapes=[
            pltpu.VMEM((14, LEN, WH), bf),
            pltpu.VMEM((LEN, 2 * GH), bf),
            pltpu.VMEM((UNITS, 2, 2, 3, QR, CH), bf),
            pltpu.VMEM((UNITS, 2, 2, 3, QR, CH), bf),
            pltpu.VMEM((UNITS, 2, 3, QR, CH), bf),
            pltpu.VMEM((UNITS, 2, 3, QR, CH), bf),
            pltpu.VMEM((UNITS, 3, QR, CH), bf),
            pltpu.VMEM((UNITS, 3, QR, CH), bf),
            pltpu.VMEM((UNITS, 3, QR, CH), bf),
            pltpu.VMEM((UNITS, 3, QR, CH), bf),
            pltpu.VMEM((UNITS, 3, QR, 2 * CH), bf),
            pltpu.VMEM((SAMES, 3, 3, QR, 2 * CH), bf),
            pltpu.VMEM((8, 3, 3, QR, 2 * CH), bf),
            pltpu.VMEM((2, 16, SEQS, 128), jnp.float32),
            dma((3,)), dma, dma, dma((3,)), dma((3,)),
            dma((3, 2)), dma((3, 2)), dma((3, 2)), dma((3, 2)), dma((3,)), dma((3,)),
            dma((2,)), dma((UNITS, 2)), dma((2,)), dma((UNITS, 2)), dma((UNITS,)), dma((SAMES,)), dma,
            dma((2,)), dma((2,)),
        ],
        compiler_params=pltpu.CompilerParams(
            collective_id=0, has_side_effects=True, vmem_limit_bytes=56 << 20),
        name="ghost_kernel",
    )(activations, out_grads, lengths)


def solution(mesh):
    placed = (P("ex", "feat"), P("ex", "feat"), P("ex"))
    return jax.shard_map(
        per_device, mesh=mesh, in_specs=placed, out_specs=P("ex", None), check_vma=False
    )
```

time: 1000 us -> 121 us (0.12)
  waiting for transfers between devices: 838 us -> 0 us
  Pallas kernels: 0 us -> 119 us
  blocking collectives: 82.5 us -> 0 us
  local copies, waits for them, and re-layouts: 36.8 us -> 1.19 us
  between operations: 14.5 us -> 0.66 us
  matrix products: 12.8 us -> 0 us
    unnamed x18 -> x0, waiting for transfers between devices: 526 us -> none
    ppermute x16 -> x0, waiting for transfers between devices: 312 us -> none  [passed_along(): return lax.ppermute(value, axis, pairs)]
    pallas_call x0 -> x1, Pallas kernels: none -> 119 us  [per_device(): pl.pallas_call(body, out_shape=jax.ShapeDtypeStruct((1, SEQS), jnp.float3...]
    all_gather x1 -> x0, blocking collectives: 49 us -> none  [per_device(): tables_all = lax.all_gather(pair_values[None], 'ex', axis=0, tiled=True)]
    psum x1 -> x0, blocking collectives: 33.5 us -> none  [per_device(): pair_values = jnp.stack([lax.psum(piece, 'feat') for piece in partials])]
    unnamed x51 -> x1, local copies, waits for them, and re-layouts: 22.6 us -> 1.19 us
    dot_general x18 -> x0, matrix products: 12.8 us -> none  [the longest x9 9.33 us: per_device(): lax.dot_general(activations, partner_acts, contract, preferred_element_ty...]
  transfers between devices with their start and end apart: 25 -> 0, of which waited for: 20 -> 0; matrix products, arithmetic and copies ran while one was open for 3% -> 0% of each run, Pallas kernels for 0% -> 0%
where the time goes in v1:
time: 121 us
  Pallas kernels  119 us (98%)
    pallas_call x1, Pallas kernels, per_device(): pl.pallas_call(body, out_shape=jax.ShapeDtypeStruct((1, SEQS), jnp.float3...  119 us

profile of v1, /device:TPU:1, one launch (start us, length us, event | category | flops | bytes accessed | tf_op | source)
XLA Modules:
  0.0 121.1 jit_solution(10496377898127573100)
XLA Ops:
  0.7 119.2 %ghost_kernel.1 = f32[1,16]{1,0:T(1,128)} custom-call(bf16[384,1792]{1,0:T(8,128)(2,1)} %act_ref.1, bf16[384,512]{1,0:T(8,128)(2,1)} %grad_ref.1, s32[1]{0:T(128)S(6)} %copy.5.len_ref), custom_call_target="tpu_custom_call" | custom-call | tf_op jit(solution)/shard_map/ghost_kernel/pallas_call | solution.py:408
  119.9 1.2 copy.6

commit v2 on v1

--- a/solution.py
+++ b/solution.py
@@ -18,7 +18,7 @@
 QR = CH // 4
 UNITS = 37
 SAMES = 13
-LAG = 4
+LAG = 3
 NT = (((1,), (1,)), ((), ()))
 
 
@@ -193,36 +193,55 @@
         r = jnp.where(t == 3, 13, 12)
         left = jnp.where(cross, jnp.where(h == 0, o, r), left)
         right = jnp.where(cross, jnp.where(h == 0, r, o), right)
-        row_wise = cross & (t == 0) & (h == 1)
+        row_wise = (cross & (t == 0) & (h == 1)) | (co & (u == 2))
+        row = jnp.where(co, 2, j)
+        col_wise = jnp.logical_not(row_wise | co | (p < 2))
         col = jnp.where(p == 2, c, jnp.where(p == 3, 2, jnp.where(st, j, p - 27) % 3))
-        us = pick(u, (0, 1, 2))
-        for b in range(3):
-            ib = jnp.where(row_wise, j, b)
-            jb = jnp.where(row_wise, b, col)
-            ib = jnp.where(co, pick(us, ((0, 1, 1)[b], (0, 0, 1)[b], 2)), ib)
-            jb = jnp.where(co, pick(us, ((1, 0, 1)[b], (0, 2, 2)[b], b)), jb)
-            ib = jnp.where(p == 0, b, jnp.where(p == 1, (1, 2, 2)[b], ib))
-            jb = jnp.where(p == 0, b, jnp.where(p == 1, (0, 0, 1)[b], jb))
-
-            def gram(half, c0, c1):
-                return lax.dot_general(w[left + half, chunk(ib), c0:c1], w[right + half, chunk(jb), c0:c1],
+
+        def gram(rows, cols, c0, c1, halves):
+            total = None
+            for half in range(halves):
+                part = lax.dot_general(w[left + half, rows, c0:c1], w[right + half, cols, c0:c1],
                                        NT, preferred_element_type=jnp.float32)
-
-            def store(pa, qg):
-                pa, qg = pa.astype(jnp.bfloat16), qg.astype(jnp.bfloat16)
-                for a in range(2):
-                    for bb in range(2):
-                        sl = slice((2 * a + bb) * QR, (2 * a + bb + 1) * QR)
-                        xp[p, a, bb, b] = pa[sl]
-                        xq[p, bb, a, b] = qg[sl]
-
-            @pl.when(cross)
+                total = part if total is None else total + part
+            return total.astype(jnp.bfloat16)
+
+        def store(b, pa, qg):
+            for a in range(2):
+                for bb in range(2):
+                    sl = slice((2 * a + bb) * QR, (2 * a + bb + 1) * QR)
+                    xp[p, a, bb, b] = pa[sl]
+                    xq[p, bb, a, b] = qg[sl]
+
+        for halves in (1, 2):
+            mine = cross if halves == 1 else jnp.logical_not(cross)
+            whole = slice(None)
+
+            @pl.when(mine & col_wise)
             def _():
-                store(gram(0, 0, AH), gram(0, AH, WH))
-
-            @pl.when(jnp.logical_not(cross))
+                pa = gram(whole, chunk(col), 0, AH, halves)
+                qg = gram(whole, chunk(col), AH, WH, halves)
+                for b in range(3):
+                    sl = slice(b * CH, (b + 1) * CH)
+                    store(b, pa[sl], qg[sl])
+
+            @pl.when(mine & row_wise)
             def _():
-                store(gram(0, 0, AH) + gram(1, 0, AH), gram(0, AH, WH) + gram(1, AH, WH))
+                pa = gram(chunk(row), whole, 0, AH, halves)
+                qg = gram(chunk(row), whole, AH, WH, halves)
+                for b in range(3):
+                    sl = slice(b * CH, (b + 1) * CH)
+                    store(b, pa[:, sl], qg[:, sl])
+
+            @pl.when(mine & jnp.logical_not(row_wise | col_wise))
+            def _():
+                for b in range(3):
+                    ib = jnp.where(u == 0, (0, 1, 1)[b], (0, 0, 1)[b])
+                    jb = jnp.where(u == 0, (1, 0, 1)[b], (0, 2, 2)[b])
+                    ib = jnp.where(p == 0, b, jnp.where(p == 1, (1, 2, 2)[b], ib))
+                    jb = jnp.where(p == 0, b, jnp.where(p == 1, (0, 0, 1)[b], jb))
+                    store(b, gram(chunk(ib), chunk(jb), 0, AH, halves),
+                          gram(chunk(ib), chunk(jb), AH, WH, halves))
 
         start(xp.at[p, 1 - qa], rp.at[p], x1_s.at[0], x1_r.at[p, 0], device(h, y, c, xa, l))
         start(xq.at[p, 1 - qb], rq.at[p], x1_s.at[1], x1_r.at[p, 1], device(h, y, c, xb, l))

time: 121 us -> 119 us (0.983)
  Pallas kernels: 119 us -> 117 us
    pallas_call x1, Pallas kernels: 119 us -> 117 us  [per_device(): pl.pallas_call(body, out_shape=jax.ShapeDtypeStruct((1, SEQS), jnp.float3...]
where the time goes in v2:
time: 119 us; the launch traced here: 118 us
  Pallas kernels  117 us (98%)
  local copies, waits for them, and re-layouts  1.19 us (1%)
    pallas_call x1, Pallas kernels, per_device(): pl.pallas_call(body, out_shape=jax.ShapeDtypeStruct((1, SEQS), jnp.float3...  117 us

profile of v2, /device:TPU:1, one launch (start us, length us, event | category | flops | bytes accessed | tf_op | source)
XLA Modules:
  0.0 118.4 jit_solution(15758068493496091358)
XLA Ops:
  0.7 116.6 %ghost_kernel.1 = f32[1,16]{1,0:T(1,128)} custom-call(bf16[384,1792]{1,0:T(8,128)(2,1)} %act_ref.1, bf16[384,512]{1,0:T(8,128)(2,1)} %grad_ref.1, s32[1]{0:T(128)S(6)} %copy.5.len_ref), custom_call_target="tpu_custom_call" | custom-call | tf_op jit(solution)/shard_map/ghost_kernel/pallas_call | solution.py:427
  117.2 1.2 %copy.6 = f32[1,16]{1,0:T(1,128)} copy(f32[1,16]{1,0:T(1,128)} %ghost_kernel.1) | data formatting | bytes 128

commit v3 on v2

--- a/solution.py
+++ b/solution.py
@@ -384,9 +384,33 @@
     def _(s):
         keep_same(s)
 
+    def drain():
+        bytes_wait(w.at[pl.ds(0, 2)], sib_s)
+        for j in range(3):
+            bytes_wait(w.at[0, chunk(j)], far_s.at[j])
+            bytes_wait(w.at[0, chunk(j)], rf_s.at[j])
+            for s in range(2):
+                bytes_wait(w.at[pl.ds(0, 2), chunk(j)], y_s.at[j, s])
+                bytes_wait(w.at[pl.ds(0, 2), chunk(j)], fw_s.at[j, s])
+        bytes_wait(rp, x1_s.at[0])
+        bytes_wait(rq, x1_s.at[1])
+        bytes_wait(rp2, x2_s.at[0])
+        bytes_wait(rq2, x2_s.at[1])
+
+        @pl.loop(0, UNITS)
+        def _(p):
+            t, k, _ = cross_of(p)
+            here = jnp.where(is_cross(p), (k == kept) & (t == l), same_of(p) % 4 == l)
+
+            @pl.when(jnp.logical_not(here))
+            def _():
+                bytes_wait(zs.at[p], z_s.at[p])
+
     def add_up(s, me, dev_of):
         for d in range(1, 16):
             start(tb.at[s, me], tb.at[s, me], t_s.at[s], t_r.at[s], dev_of((me + d) % 16))
+        if s == 0:
+            drain()
         bytes_wait(tb.at[s, pl.ds(0, 15)], t_r.at[s])
         total = tb[s, 0]
         for d in range(1, 16):
@@ -398,28 +422,8 @@
     line = jnp.sum(jnp.where(row_id == e, total, 0.0), axis=0, keepdims=True)
     out_ref[...] = line[:, 0:SEQS] / float(LEN * FF * D)
 
-    bytes_wait(w.at[pl.ds(0, 2)], sib_s)
-    for j in range(3):
-        bytes_wait(w.at[0, chunk(j)], far_s.at[j])
-        bytes_wait(w.at[0, chunk(j)], rf_s.at[j])
-        for s in range(2):
-            bytes_wait(w.at[pl.ds(0, 2), chunk(j)], y_s.at[j, s])
-            bytes_wait(w.at[pl.ds(0, 2), chunk(j)], fw_s.at[j, s])
     for s in range(2):
         bytes_wait(tb.at[s, pl.ds(0, 15)], t_s.at[s])
-    bytes_wait(rp, x1_s.at[0])
-    bytes_wait(rq, x1_s.at[1])
-    bytes_wait(rp2, x2_s.at[0])
-    bytes_wait(rq2, x2_s.at[1])
-
-    @pl.loop(0, UNITS)
-    def _(p):
-        t, k, _ = cross_of(p)
-        here = jnp.where(is_cross(p), (k == kept) & (t == l), same_of(p) % 4 == l)
-
-        @pl.when(jnp.logical_not(here))
-        def _():
-            bytes_wait(zs.at[p], z_s.at[p])
 
 
 def per_device(activations, out_grads, lengths):

time: 119 us -> 117 us (0.983)
  Pallas kernels: 117 us -> 115 us
    pallas_call x1, Pallas kernels: 117 us -> 115 us  [per_device(): pl.pallas_call(body, out_shape=jax.ShapeDtypeStruct((1, SEQS), jnp.float3...]
where the time goes in v3:
time: 117 us
  Pallas kernels  115 us (98%)
  local copies, waits for them, and re-layouts  1.19 us (1%)
    pallas_call x1, Pallas kernels, per_device(): pl.pallas_call(body, out_shape=jax.ShapeDtypeStruct((1, SEQS), jnp.float3...  115 us

profile of v3, /device:TPU:1, one launch (start us, length us, event | category | flops | bytes accessed | tf_op | source)
XLA Modules:
  0.0 116.5 jit_solution(2286089259095588414)
XLA Ops:
  0.7 114.7 %ghost_kernel.1 = f32[1,16]{1,0:T(1,128)} custom-call(bf16[384,1792]{1,0:T(8,128)(2,1)} %act_ref.1, bf16[384,512]{1,0:T(8,128)(2,1)} %grad_ref.1, s32[1]{0:T(128)S(6)} %copy.5.len_ref), custom_call_target="tpu_custom_call" | custom-call | tf_op jit(solution)/shard_map/ghost_kernel/pallas_call | solution.py:431
  115.3 1.2 %copy.6 = f32[1,16]{1,0:T(1,128)} copy(f32[1,16]{1,0:T(1,128)} %ghost_kernel.1) | data formatting | bytes 128

commit v4 on v3

--- a/solution.py
+++ b/solution.py
@@ -140,13 +140,15 @@
 
         start(w.at[12, chunk(j)], w.at[13, chunk(j)], rf_s.at[j], rf_r.at[j],
               device(h, jnp.where(c == 0, down, up), c, x, l))
+
+    def arrive_passed(j):
         for s in range(2):
             slot = pl.ds((8 if s == 0 else 0) + 2 * (1 - c), 2)
             bytes_wait(w.at[slot, chunk(j)], fw_r.at[j, s])
 
     def stage_of(p):
         j = jnp.where(p < 8, 0, jnp.where(p < 17, 1, 2))
-        return j, jnp.where(p > 32, p - 33, p - pick(j, (4, 8, 15)))
+        return j, jnp.where(p > 32, p - 33, jnp.where(p > 16, p - 15, (p + 2) % 4))
 
     def corner(p):
         late = p > 34
@@ -178,7 +180,7 @@
 
     def unit_of_same(s):
         j, q = (s - 4) // 2, (s - 4) % 2
-        return jnp.where(s < 4, s, jnp.where(s < 10, pick(j, (4, 8, 33)) + q,
+        return jnp.where(s < 4, s, jnp.where(s < 10, pick(j, (6, 10, 33)) + q,
                                              pick(s - 10, (12, 35, 36))))
 
     def multiply(p):
@@ -332,6 +334,10 @@
         @pl.when((p == 4) | (p == 8) | (p == 17))
         def _():
             arrive(stage_of(p)[0])
+
+        @pl.when((p == 6) | (p == 10) | (p == 19))
+        def _():
+            arrive_passed(jnp.where(p == 6, 0, jnp.where(p == 10, 1, 2)))
 
         @pl.when(p == 27)
         def _():

time: 117 us -> 116 us (level)
  no operation moved by 1% of the time
where the time goes in v4:
time: 116 us; the launch traced here: 115 us
  Pallas kernels  114 us (98%)
  local copies, waits for them, and re-layouts  1.19 us (1%)
    pallas_call x1, Pallas kernels, per_device(): pl.pallas_call(body, out_shape=jax.ShapeDtypeStruct((1, SEQS), jnp.float3...  114 us

profile of v4, /device:TPU:1, one launch (start us, length us, event | category | flops | bytes accessed | tf_op | source)
XLA Modules:
  0.0 115.4 jit_solution(14464751830059592585)
XLA Ops:
  0.7 113.6 %ghost_kernel.1 = f32[1,16]{1,0:T(1,128)} custom-call(bf16[384,1792]{1,0:T(8,128)(2,1)} %act_ref.1, bf16[384,512]{1,0:T(8,128)(2,1)} %grad_ref.1, s32[1]{0:T(128)S(6)} %copy.5.len_ref), custom_call_target="tpu_custom_call" | custom-call | tf_op jit(solution)/shard_map/ghost_kernel/pallas_call | solution.py:437
  114.2 1.2 %copy.6 = f32[1,16]{1,0:T(1,128)} copy(f32[1,16]{1,0:T(1,128)} %ghost_kernel.1) | data formatting | bytes 128
